TPU v7x, 32 devices: a whole 2x2x4 slice. The times are simulated.
32 devices in a mesh: img: 8 (over y, x, core), pw: 4 (over z).
Axes of the slice: x: 2, y: 2, z: 4, core: 2. Of those that a mesh axis runs over, the one named last changes fastest.
Arguments:
- band_panel: bfloat16 [1024, 57344], P(None, 'pw'), may hold values from -0.0793431812 to 0.0793431812
- gsphere: int32 [57344], P('pw'), may hold values from 0 to 65535, as said below
- eps_band: float32 [2], replicated, may hold values from -2 to -0.5
- local_pot: float32 [64, 4096], P('pw'), may hold values from 0.5 to 3
- dvpert: bfloat16 [128, 64, 4096], P('img', 'pw'), may hold values from -6 to 6
- beta_proj: float32 [4096, 128], P('pw'), may hold values from -1.5 to 1.5
- proj_coef: float32 [4096], P('pw'), may hold values from 0.5 to 2
- pblock: int32 [4096], P('pw'), may hold values from 0 to 511
Outputs:
- density_resp: float32 [128, 64, 4096], P('img', 'pw')
- chi_matrix: float32 [128, 128], P(None, 'img')
Inputs may be any that keep to these rules, and one draw needn't show every extreme that they name: `gsphere`: each group of 14336 consecutive entries names distinct cells of the frequency slab of 64 x 16 x 64 cells of that group, in ascending order, always including its first and last cell. `pblock`: entry p counts blocks of 128 cells from the start of the grid slab of group p // 1024.
All inputs are finite; a program needn't handle non-finite values.
Results may differ from a plain program's by a relative error of at most 0.0035.
The roundings to bfloat16 on the way count: a program that leaves them out, or rounds other values in their place, can miss the bound.
Values may be sent and summed in bfloat16 or wider, within the bound.
A program may use at most 192 MiB of HBM per device.

v0:
```python
import math

import jax
import jax.numpy as jnp
from jax import lax
from jax.sharding import PartitionSpec as P

N = 64
NB = 2
ITERS = 2


ALPHA_PV = 2.0
SHIFT_EPS = 1e-06
HIGHEST = lax.Precision.HIGHEST


def cas_table(length):
    idx_line = jnp.arange(length, dtype=jnp.int32)
    product = idx_line[:, None] * idx_line[None, :] % length
    angle = product.astype(jnp.float32) * (2.0 * math.pi / length)
    return jnp.cos(angle) + jnp.sin(angle)


def frequency(index_vals, length):
    return jnp.where(index_vals < length // 2, index_vals, index_vals - length).astype(jnp.float32)


def local(band_panel, gsphere, eps_band, local_pot, dvpert, beta_proj, proj_coef, pblock):
    points = N
    slab_rows = local_pot.shape[0]
    plane_size = points * points
    cas_rows = cas_table(points)
    scaled_rows = cas_rows / points
    pw_rank = lax.axis_index("pw")
    freq_x = gsphere // (slab_rows * points)
    freq_y = pw_rank * slab_rows + gsphere // points % slab_rows
    freq_z = gsphere % points
    kx_val = frequency(freq_x, points)
    ky_val = frequency(freq_y, points)
    kz_val = frequency(freq_z, points)
    kinetic = 8.0 * (kx_val * kx_val + ky_val * ky_val + kz_val * kz_val) / (points * points)

    def to_real(coeffs):
        batch_size = coeffs.shape[0]
        freq_box = (
            jnp.zeros((batch_size, points * slab_rows * points), jnp.float32)
            .at[:, gsphere]
            .set(coeffs)
        )
        freq_box = freq_box.reshape(batch_size, points, slab_rows, points)
        along_x = jnp.einsum("wgyz,gx->wxyz", freq_box, cas_rows, precision=HIGHEST)
        pieces = lax.all_to_all(along_x, "pw", split_axis=1, concat_axis=2, tiled=True)
        partial_value = jnp.einsum("wxgz,gy->wxyz", pieces, cas_rows, precision=HIGHEST)
        partial_value = jnp.einsum("wxyg,gz->wxyz", partial_value, cas_rows, precision=HIGHEST)
        return partial_value.reshape(pieces.shape[0], slab_rows, plane_size)

    def to_sphere(field_in):
        batch_size = field_in.shape[0]
        cube_cells = field_in.reshape(batch_size, slab_rows, points, points)
        partial_value = jnp.einsum("wxyz,yg->wxgz", cube_cells, scaled_rows, precision=HIGHEST)
        partial_value = jnp.einsum("wxgz,zh->wxgh", partial_value, scaled_rows, precision=HIGHEST)
        pieces = lax.all_to_all(partial_value, "pw", split_axis=2, concat_axis=1, tiled=True)
        whole_box = jnp.einsum("wxgh,xf->wfgh", pieces, scaled_rows, precision=HIGHEST)
        return whole_box.reshape(pieces.shape[0], points * slab_rows * points)[:, gsphere]

    def correlation_part(coeffs):
        return lax.dot_general(
            coeffs.astype(jnp.bfloat16),
            band_panel,
            (((1,), (1,)), ((), ())),
            preferred_element_type=jnp.float32,
        )

    def correlations(coeffs):
        return lax.psum(correlation_part(coeffs), "pw")

    def residual_norm(residual):
        return lax.psum(jnp.sum(residual * residual, axis=1), "pw")

    pert_dev = dvpert.shape[0]
    batch_rows = pert_dev * NB
    bands_real = to_real(band_panel[:NB].astype(jnp.float32))
    products = dvpert.astype(jnp.float32)[:, None] * bands_real[None]
    source = to_sphere(products.reshape(batch_rows, slab_rows, plane_size))
    source_over = correlations(source).astype(jnp.bfloat16)
    right_side = jnp.dot(source_over, band_panel, preferred_element_type=jnp.float32) - source
    eps_rows = jnp.tile(eps_band, pert_dev)
    solution = jnp.zeros_like(right_side)
    residual = right_side
    direction = right_side
    norm_now = residual_norm(residual)
    for iteration in range(ITERS):
        correlation = correlations(direction)
        field_real = to_real(direction)
        nonlocal_batch_size = field_real.shape[0]
        blocks = field_real.reshape(
            nonlocal_batch_size, slab_rows * plane_size // beta_proj.shape[1], beta_proj.shape[1]
        )
        picked = blocks[:, pblock, :]
        proj_amp = jnp.sum(picked * beta_proj[None], axis=2) * proj_coef[None]
        addition = proj_amp[:, :, None] * beta_proj[None]
        potential = local_pot[None] * field_real + jnp.zeros_like(blocks).at[:, pblock, :].add(
            addition
        ).reshape(field_real.shape)
        applied, field_real = (kinetic[None] * direction + to_sphere(potential), field_real)
        shifted = applied - eps_rows[:, None] * direction
        curvature = lax.psum(jnp.sum(direction * shifted, axis=1), "pw")
        over_b = correlation.astype(jnp.bfloat16)
        curvature = curvature + ALPHA_PV * jnp.sum(correlation * over_b.astype(jnp.float32), axis=1)
        product_vec = shifted + ALPHA_PV * jnp.dot(
            over_b, band_panel, preferred_element_type=jnp.float32
        )
        step_len = norm_now / curvature
        solution = solution + step_len[:, None] * direction
        residual = residual - step_len[:, None] * product_vec
        if iteration + 1 < ITERS:
            norm_next = residual_norm(residual)
            direction = residual + (norm_next / (norm_now + SHIFT_EPS))[:, None] * direction
            norm_now = norm_next
    change = to_real(solution)
    density_resp = 4.0 * jnp.sum(
        bands_real[None] * change.reshape(pert_dev, NB, slab_rows, plane_size), axis=1
    )
    flat_rho = density_resp.reshape(pert_dev, slab_rows * plane_size)
    shard_in = lax.all_gather(dvpert, "img", axis=0, tiled=True)
    values = shard_in.reshape(shard_in.shape[0], slab_rows * plane_size).astype(jnp.float32)
    block_vals = lax.dot_general(
        values,
        flat_rho,
        (((1,), (1,)), ((), ())),
        precision=HIGHEST,
        preferred_element_type=jnp.float32,
    )
    chi_matrix = lax.psum(block_vals, "pw") / (points * points * points)
    return (density_resp, chi_matrix)


def solution(mesh):
    return jax.shard_map(
        local,
        mesh=mesh,
        in_specs=(
            P(None, "pw"),
            P("pw"),
            P(),
            P("pw", None),
            P("img", "pw", None),
            P("pw", None),
            P("pw"),
            P("pw"),
        ),
        out_specs=(P("img", "pw", None), P(None, "img")),
        check_vma=False,
    )
```

profile of v0, /device:TPU:0, one launch (start us, length us, event | category | flops | bytes accessed | tf_op | source)
XLA Modules:
  0.0 3301.6 jit_solution(16830966775376373453)
XLA Ops:
  14.3 48.9 %scatter_custom_fusion = f32[2,65536]{0,1:T(8,128)} fusion(s32[14336]{0:T(1024)S(1)} %get-tuple-element.7, f32[14336,2]{1,0:T(8,128)} %copy.119, f32[]{:T(128)} %constant.81.clone.1), kind=kCustom, calls=%fused_computation.39 | custom fusion | bytes 524800 | tf_op jit(solution)/shard_map/scatter | solution.py:49
  63.2 20.2 copy.121
  134.5 21.9 fusion.72
  156.4 23.6 fusion.10
  213.7 190.2 %all_to_all.128 = f32[4,1,524288]{2,1,0:T(1,128)} all-to-all(f32[4,1,524288]{2,1,0:T(1,128)} %reshape.216), channel_id=1, replica_groups=mesh['img'=8,'pw'=4] {'pw'}, dimensions={0} | all-to-all | bytes 16777216 | tf_op jit(solution)/shard_map/all_to_all | solution.py:63
  403.8 28.2 reduce.5
  460.7 21.9 convolution_bitcast_fusion.5
  482.6 23.8 copy.197
  506.4 58.3 %gather_fusion = f32[14336,32]{1,0:T(8,128)} fusion(f32[32,65536]{0,1:T(8,128)} %bitcast.243, s32[14336]{0:T(1024)S(1)} %get-tuple-element.6), kind=kCustom, calls=%fused_computation | custom fusion | bytes 3727360 | tf_op jit(solution)/shard_map/gather | solution.py:65
  620.6 49.0 %scatter_custom_fusion.1 = f32[32,65536]{0,1:T(8,128)} fusion(s32[14336]{0:T(1024)S(1)} %get-tuple-element.7, f32[14336,32]{1,0:T(8,128)} %copy.133, f32[]{:T(128)} %constant.81.clone.1), kind=kCustom, calls=%fused_computation.37 | custom fusion | bytes 8389120 | tf_op jit(solution)/shard_map/scatter | solution.py:49
  669.6 26.1 copy.135
  695.7 21.7 convolution_bitcast_fusion.4
  754.0 178.9 %all-to-all-done.2 = f32[4,1,524288]{2,1,0:T(1,128)} async-done(((f32[4,1,524288]{2,1,0:T(1,128)}), f32[4,1,524288]{2,1,0:T(1,128)}, u32[]{:S(2)}, u32[]{:S(2)}) %all-to-all-start.2) | async-done | bytes 8388640 | tf_op jit(solution)/shard_map/all_to_all | solution.py:53
  932.8 28.2 reduce.6
  989.9 21.7 fusion.79
  1093.6 134.5 %scatter_fusion = f32[32,512,128]{2,0,1:T(8,128)} fusion(f32[32,512,128]{2,0,1:T(8,128)} %broadcast.88.clone, s32[1024]{0:T(1024)S(1)} %get-tuple-element.9, f32[1024,32,128]{2,1,0:T(8,128)} %multiply_bitcast_fusion.1), kind=kCustom, calls=%fused_computation.7 | custom fusion | flops 4194304 | bytes 50335744 | tf_op jit(solution)/shard_map/scatter-add | solution.py:103
  1252.3 24.3 fusion.15
  1276.6 23.3 fusion.6
  1299.9 19.3 copy.228
  1355.0 62.1 %all-reduce.5.cloned.1.call-done = f32[32,1024]{1,0:T(8,128)} async-done(((f32[32,1024]{1,0:T(8,128)}), f32[32,1024]{1,0:T(8,128)}) %all-reduce.5.cloned.1.call-update) | async-done | bytes 131088 | tf_op jit(solution)/shard_map/psum | solution.py:76
  1418.1 108.0 %all-to-all-done.3 = f32[4,1,524288]{2,1,0:T(1,128)} async-done(((f32[4,1,524288]{2,1,0:T(1,128)}), f32[4,1,524288]{2,1,0:T(1,128)}, u32[]{:S(2)}, u32[]{:S(2)}) %all-to-all-start.3) | async-done | bytes 8388640 | tf_op jit(solution)/shard_map/all_to_all | solution.py:63
  1526.2 28.2 reduce.7
  1583.0 21.8 convolution_bitcast_fusion.3
  1604.9 23.8 copy.203
  1628.7 58.4 %gather_fusion.2 = f32[14336,32]{1,0:T(8,128)} fusion(f32[32,65536]{0,1:T(8,128)} %bitcast.245, s32[14336]{0:T(1024)S(1)} %copy-done.15), kind=kCustom, calls=%fused_computation.2 | custom fusion | bytes 3727360 | tf_op jit(solution)/shard_map/gather | solution.py:65
  1739.2 48.8 %scatter_custom_fusion.3 = f32[32,65536]{0,1:T(8,128)} fusion(s32[14336]{0:T(1024)} %copy-done.20, f32[14336,32]{1,0:T(8,128)} %copy.149, f32[]{:T(128)} %constant.81.clone.1), kind=kCustom, calls=%fused_computation.35 | custom fusion | bytes 8389120 | tf_op jit(solution)/shard_map/scatter | solution.py:49
  1788.1 26.5 copy.151
  1814.5 21.7 convolution_bitcast_fusion.2
  1866.5 186.5 %all_to_all.126 = f32[4,1,524288]{2,1,0:T(1,128)} all-to-all(f32[4,1,524288]{2,1,0:T(1,128)} %reshape.222), channel_id=1, replica_groups=mesh['img'=8,'pw'=4] {'pw'}, dimensions={0} | all-to-all | bytes 16777216 | tf_op jit(solution)/shard_map/all_to_all | solution.py:53
  2053.0 28.2 reduce.8
  2109.9 21.9 fusion.76
  2214.0 134.4 %scatter_fusion.1 = f32[32,512,128]{2,0,1:T(8,128)} fusion(f32[32,512,128]{2,0,1:T(8,128)} %broadcast.88, s32[1024]{0:T(1024)S(1)} %copy-done.22, f32[1024,32,128]{2,1,0:T(8,128)} %multiply_bitcast_fusion), kind=kCustom, calls=%fused_computation.9 | custom fusion | flops 4194304 | bytes 50335744 | tf_op jit(solution)/shard_map/scatter-add | solution.py:103
  2372.7 24.0 fusion.12
  2396.7 23.4 fusion.2
  2420.2 19.3 copy.226
  2459.7 26.3 fusion.43
  2490.1 44.9 %all-reduce.7.cloned.1.call-done = f32[32,1024]{1,0:T(8,128)} async-done(((f32[32,1024]{1,0:T(8,128)}), f32[32,1024]{1,0:T(8,128)}) %all-reduce.7.cloned.1.call-update) | async-done | bytes 131088 | tf_op jit(solution)/shard_map/psum | solution.py:76
  2536.2 108.5 %all-to-all-done.5 = f32[4,1,524288]{2,1,0:T(1,128)} async-done(((f32[4,1,524288]{2,1,0:T(1,128)}), f32[4,1,524288]{2,1,0:T(1,128)}, u32[]{:S(2)}, u32[]{:S(2)}) %all-to-all-start.5) | async-done | bytes 8388640 | tf_op jit(solution)/shard_map/all_to_all | solution.py:63
  2644.6 28.2 reduce.9
  2701.5 21.9 convolution_bitcast_fusion.1
  2723.4 23.8 copy.209
  2747.2 58.5 %gather_fusion.4 = f32[14336,32]{1,0:T(8,128)} fusion(f32[32,65536]{0,1:T(8,128)} %bitcast.244, s32[14336]{0:T(1024)S(1)} %copy-done.16), kind=kCustom, calls=%fused_computation.4 | custom fusion | bytes 3727360 | tf_op jit(solution)/shard_map/gather | solution.py:65
  2832.9 48.8 %scatter_custom_fusion.5 = f32[32,65536]{0,1:T(8,128)} fusion(s32[14336]{0:T(1024)} %copy-done.20, f32[14336,32]{1,0:T(8,128)} %copy.165, f32[]{:T(128)} %constant.81.clone.1), kind=kCustom, calls=%fused_computation.33 | custom fusion | bytes 8389120 | tf_op jit(solution)/shard_map/scatter | solution.py:49
  2881.8 26.2 copy.167
  2908.0 21.7 convolution_bitcast_fusion
  2959.9 187.2 %all_to_all.127 = f32[4,1,524288]{2,1,0:T(1,128)} all-to-all(f32[4,1,524288]{2,1,0:T(1,128)} %reshape.226), channel_id=1, replica_groups=mesh['img'=8,'pw'=4] {'pw'}, dimensions={0} | all-to-all | bytes 16777216 | tf_op jit(solution)/shard_map/all_to_all | solution.py:53
  3147.1 28.2 reduce.10
  3204.0 21.8 fusion.82
  (176 shorter events, 838.3 us)
Async XLA Ops:
  8.8 497.6 %copy-start.14 = (s32[14336]{0:T(1024)}, s32[14336]{0:T(1024)S(1)}, u32[]{:S(2)}) copy-start(s32[14336]{0:T(1024)S(1)} %get-tuple-element.6) | copy-start | bytes 172036
  8.8 611.7 %copy-start.20 = (s32[14336]{0:T(1024)}, s32[14336]{0:T(1024)S(1)}, u32[]{:S(2)}) copy-start(s32[14336]{0:T(1024)S(1)} %get-tuple-element.7) | copy-start | bytes 172036
  63.2 30.0 copy-start.7
  86.6 21.0 all-to-all-start
  113.6 20.8 copy-start.10
  569.7 14.8 copy-start.4
  616.1 53.5 %copy-start = (f32[32,14336]{1,0:T(8,128)}, f32[32,14336]{1,0:T(8,128)S(1)}, u32[]{:S(2)}) copy-start(f32[32,14336]{1,0:T(8,128)S(1)} %convolution_subtract_fusion) | copy-start | bytes 5505028
  733.3 20.4 copy-start.18
  733.3 20.6 copy-start.31
  748.0 184.8 %all-to-all-start.2 = ((f32[4,1,524288]{2,1,0:T(1,128)}), f32[4,1,524288]{2,1,0:T(1,128)}, u32[]{:S(2)}, u32[]{:S(2)}) async-start(f32[4,1,524288]{2,1,0:T(1,128)} %reshape.218), calls=%async_computation.2 | async-start | bytes 16777216 | tf_op jit(solution)/shard_map/all_to_all | solution.py:53
  753.9 498.4 %copy-start.8 = (f32[16,64,64]{2,1,0:T(8,128)}, f32[16,64,64]{2,1,0:T(8,128)S(1)}, u32[]{:S(2)}) copy-start(f32[16,64,64]{2,1,0:T(8,128)S(1)} %mul.407) | copy-start | bytes 786436
  753.9 301.7 %copy-start.23 = (s32[1024]{0:T(1024)}, s32[1024]{0:T(1024)S(1)}, u32[]{:S(2)}) copy-start(s32[1024]{0:T(1024)S(1)} %get-tuple-element.8) | copy-start | bytes 12292
  753.9 339.7 %copy-start.21 = (s32[1024]{0:T(1024)}, s32[1024]{0:T(1024)S(1)}, u32[]{:S(2)}) copy-start(s32[1024]{0:T(1024)S(1)} %get-tuple-element.9) | copy-start | bytes 12292
  1055.6 15.9 copy-start.5
  1071.5 8.2 copy-start.25
  1319.2 20.2 copy-start.1
  1333.7 192.4 %all-to-all-start.3 = ((f32[4,1,524288]{2,1,0:T(1,128)}), f32[4,1,524288]{2,1,0:T(1,128)}, u32[]{:S(2)}, u32[]{:S(2)}) async-start(f32[4,1,524288]{2,1,0:T(1,128)} %reshape.220), calls=%async_computation.3 | async-start | bytes 16777216 | tf_op jit(solution)/shard_map/all_to_all | solution.py:63
  1339.4 77.7 %all-reduce.5.cloned.1.call-start = ((), (), s32[]{:S(2)}) async-start(), calls=%async_computation.7 | async-start | bytes 262144 | tf_op jit(solution)/shard_map/psum | solution.py:76
  1339.4 15.2 copy-start.19
  1339.5 15.4 copy-start.32
  1354.8 350.4 %copy-start.12 = (f32[14336]{0:T(1024)}, f32[14336]{0:T(1024)S(1)}, u32[]{:S(2)}) copy-start(f32[14336]{0:T(1024)S(1)} %fusion.55) | copy-start | bytes 172036
  1355.0 350.3 %copy-start.27 = (f32[32]{0:T(128)}, f32[32]{0:T(128)S(1)}, u32[]{:S(2)}) copy-start(f32[32]{0:T(128)S(1)} %mul.416) | copy-start | bytes 388
  1604.9 23.8 copy-start.15
  1628.7 76.6 %copy-start.17 = (f32[32,1024]{1,0:T(8,128)S(1)}, f32[32,1024]{1,0:T(8,128)}, u32[]{:S(2)}) copy-start(f32[32,1024]{1,0:T(8,128)} %all-reduce.5.cloned.1.call-done) | copy-start | bytes 393220
  1705.3 16.7 copy-start.29
  1730.9 57.2 %copy-start.33 = (f32[32]{0:T(128)}, f32[32]{0:T(128)S(1)}, u32[]{:S(2)}) copy-start(f32[32]{0:T(128)S(1)} %psum.60) | copy-start | bytes 388
  2150.5 25.6 copy-start.24
  2176.0 15.9 copy-start.6
  2191.9 8.2 copy-start.26
  2200.1 13.9 copy-start.22
  2359.8 12.9 copy-start.9
  2439.5 20.2 copy-start.3
  2454.0 190.6 %all-to-all-start.5 = ((f32[4,1,524288]{2,1,0:T(1,128)}), f32[4,1,524288]{2,1,0:T(1,128)}, u32[]{:S(2)}, u32[]{:S(2)}) async-start(f32[4,1,524288]{2,1,0:T(1,128)} %reshape.224), calls=%async_computation.5 | async-start | bytes 16777216 | tf_op jit(solution)/shard_map/all_to_all | solution.py:63
  2459.6 75.4 %all-reduce.7.cloned.1.call-start = ((), (), s32[]{:S(2)}) async-start(), calls=%async_computation.8 | async-start | bytes 262144 | tf_op jit(solution)/shard_map/psum | solution.py:76
  2486.0 780.9 %all-gather.2.cloned.1.call-start = ((), (), s32[]{:S(2)}) async-start(), calls=%async_computation.9 | async-start | bytes 18874368 | tf_op jit(solution)/shard_map/all_gather | solution.py:126
  2723.4 23.9 copy-start.16
  2747.2 64.6 %copy-start.13 = (f32[14336]{0:T(1024)S(1)}, f32[14336]{0:T(1024)}, u32[]{:S(2)}) copy-start(f32[14336]{0:T(1024)} %copy-done.12) | copy-start | bytes 172036
  2747.2 64.6 %copy-start.28 = (f32[32]{0:T(128)S(1)}, f32[32]{0:T(128)}, u32[]{:S(2)}) copy-start(f32[32]{0:T(128)} %copy-done.27) | copy-start | bytes 388
  2747.2 77.3 %copy-start.34 = (f32[32]{0:T(128)S(1)}, f32[32]{0:T(128)}, u32[]{:S(2)}) copy-start(f32[32]{0:T(128)} %copy-done.33) | copy-start | bytes 388
  2747.2 77.3 %copy-start.2 = (f32[32,14336]{1,0:T(8,128)S(1)}, f32[32,14336]{1,0:T(8,128)}, u32[]{:S(2)}) copy-start(f32[32,14336]{1,0:T(8,128)} %copy-done) | copy-start | bytes 5505028
  2747.2 77.3 %copy-start.30 = (f32[32]{0:T(128)S(1)}, f32[32]{0:T(128)}, u32[]{:S(2)}) copy-start(f32[32]{0:T(128)} %copy-done.29) | copy-start | bytes 388
  3244.6 15.0 copy-start.11
Sparse Core Ops, SparseCore 0:
  1354.8 62.1 all-reduce.4
  2486.1 48.9 all-reduce.6
Sparse Core Ops, SparseCore 1:
  2490.2 91.0 all-gather.1
where the time goes:
time: 3320 us; the launch traced here: 3300 us
  local copies, waits for them, and re-layouts  1120 us (34%)
  blocking collectives  622 us (19%)
  waiting for transfers between devices  514 us (15%)
  other arithmetic  508 us (15%)
  matrix products  498 us (15%)
    all_to_all x2, blocking collectives, to_real(): lax.all_to_all(along_x, 'pw', split_axis=1, concat_axis=2, tiled=True)  374 us
    scatter-add x2, other arithmetic, local(): jnp.zeros_like(blocks).at[:, pblock, :].add(addition)  269 us
    all_to_all x2, waiting for transfers between devices, to_sphere(): lax.all_to_all(partial_value, 'pw', split_axis=2, concat_axis=1, tiled=True)  216 us
    scatter x4, local copies, waits for them, and re-layouts, to_real(): freq_box = jnp.zeros((batch_size, points * slab_rows * points), jnp.float...  196 us
    unnamed x85, local copies, waits for them, and re-layouts  193 us
    gather x6, local copies, waits for them, and re-layouts, to_sphere(): whole_box.reshape(pieces.shape[0], points * slab_rows * points)[:, gsphere]  192 us
    all_to_all x2, waiting for transfers between devices, to_real(): lax.all_to_all(along_x, 'pw', split_axis=1, concat_axis=2, tiled=True)  191 us
    all_to_all x1, blocking collectives, to_sphere(): lax.all_to_all(partial_value, 'pw', split_axis=2, concat_axis=1, tiled=True)  190 us
  transfers between devices with their start and end apart: 7, of which 6 were waited for; matrix products, arithmetic and copies ran while one was open for 14% of the time, Pallas kernels for 0%

commit v1 on v0

--- a/solution.py
+++ b/solution.py
@@ -3,6 +3,8 @@
 import jax
 import jax.numpy as jnp
 from jax import lax
+from jax.experimental import pallas as pl
+from jax.experimental.pallas import tpu as pltpu
 from jax.sharding import PartitionSpec as P
 
 N = 64
@@ -26,7 +28,7 @@
     return jnp.where(index_vals < length // 2, index_vals, index_vals - length).astype(jnp.float32)
 
 
-def local(band_panel, gsphere, eps_band, local_pot, dvpert, beta_proj, proj_coef, pblock):
+def slab_plan(band_panel, gsphere, eps_band, local_pot, dvpert, beta_proj, proj_coef, pblock):
     points = N
     slab_rows = local_pot.shape[0]
     plane_size = points * points
@@ -136,6 +138,287 @@
     return (density_resp, chi_matrix)
 
 
+SENT = jnp.bfloat16
+MID = lax.Precision.HIGH
+
+
+LANES = 128
+STEP_X = 8
+VMEM_BYTES = 40 * 1024 * 1024
+
+
+def swap_lines(tile):
+    rows, lanes = tile.shape
+    turned = pltpu.roll(pltpu.roll(tile, rows // 2, 0), lanes // 2, 1)
+    low_lane = lax.broadcasted_iota(jnp.int32, tile.shape, 1) < lanes // 2
+    low_row = lax.broadcasted_iota(jnp.int32, tile.shape, 0) < rows // 2
+    return jnp.where(low_lane == low_row, tile, turned)
+
+
+def pick_lanes(tile, index):
+    return jnp.take_along_axis(tile, index & (LANES - 1), axis=1, mode="promise_in_bounds")
+
+
+def expand_kernel(base_ref, place_ref, coeffs_ref, out_ref):
+    pairs = out_ref.shape[1]
+    first = pl.program_id(0) * STEP_X
+
+    def body(step, carry):
+        x, pair = step // pairs, step % pairs
+        base = pl.multiple_of(base_ref[first + x, pair], LANES)
+        index = jnp.broadcast_to(place_ref[x, pl.ds(pair, 1), :], (8, LANES))
+        head = pick_lanes(coeffs_ref[:, pl.ds(base, LANES)], index)
+        tail = pick_lanes(coeffs_ref[:, pl.ds(base + LANES, LANES)], index)
+        found = jnp.where(index < LANES, head, tail)
+        out_ref[x, pair] = swap_lines(jnp.where(index < 0, 0.0, found))
+        return carry
+
+    lax.fori_loop(0, STEP_X * pairs, body, 0, unroll=8)
+
+
+def compress_kernel(base_ref, block_ref, entry_ref, box_ref, out_ref):
+    pairs = box_ref.shape[1]
+    first = pl.program_id(0) * STEP_X
+
+    def body(step, carry):
+        x, pair = step // pairs, step % pairs
+        base = pl.multiple_of(base_ref[first + x, pair], LANES)
+        tile = swap_lines(box_ref[x, pair])
+        for shift in (0, LANES):
+            window = pl.ds(base + shift, LANES)
+            index = entry_ref[:, window] - block_ref[first + x, pair] * LANES
+            inside = (index >= 0) & (index < LANES)
+            out_ref[:, window] = jnp.where(inside, pick_lanes(tile, index), out_ref[:, window])
+        return carry
+
+    lax.fori_loop(0, STEP_X * pairs, body, 0, unroll=4)
+
+
+def expand(base, place, coeffs):
+    points, pairs = base.shape
+    return pl.pallas_call(
+        expand_kernel,
+        grid=(points // STEP_X,),
+        in_specs=[
+            pl.BlockSpec(memory_space=pltpu.SMEM),
+            pl.BlockSpec((STEP_X, pairs, LANES), lambda i: (i, 0, 0)),
+            pl.BlockSpec(coeffs.shape, lambda i: (0, 0)),
+        ],
+        out_specs=pl.BlockSpec((STEP_X, pairs, 8, LANES), lambda i: (i, 0, 0, 0)),
+        out_shape=jax.ShapeDtypeStruct((points, pairs, 8, LANES), jnp.float32),
+        compiler_params=pltpu.CompilerParams(vmem_limit_bytes=VMEM_BYTES),
+    )(base, place, coeffs)
+
+
+def compress(base, block, entries, box):
+    points, pairs = base.shape
+    return pl.pallas_call(
+        compress_kernel,
+        grid=(points // STEP_X,),
+        in_specs=[
+            pl.BlockSpec(memory_space=pltpu.SMEM),
+            pl.BlockSpec(memory_space=pltpu.SMEM),
+            pl.BlockSpec(entries.shape, lambda i: (0, 0)),
+            pl.BlockSpec((STEP_X, pairs, 8, LANES), lambda i: (i, 0, 0, 0)),
+        ],
+        out_specs=pl.BlockSpec(entries.shape, lambda i: (0, 0)),
+        out_shape=jax.ShapeDtypeStruct(entries.shape, jnp.float32),
+        compiler_params=pltpu.CompilerParams(vmem_limit_bytes=VMEM_BYTES),
+    )(base, block, entries, box)
+
+
+def local(band_panel, gsphere, eps_band, local_pot, dvpert, beta_proj, proj_coef, pblock):
+    ranks = lax.axis_size("pw")
+    pert_dev = dvpert.shape[0]
+    if pert_dev % ranks or pert_dev // ranks * NB != 8 or gsphere.shape[0] % LANES:
+        return slab_plan(
+            band_panel, gsphere, eps_band, local_pot, dvpert, beta_proj, proj_coef, pblock
+        )
+    points = N
+    slab_rows = local_pot.shape[0]
+    lanes = NB * points
+    perts = pert_dev // ranks
+    sphere_dev = gsphere.shape[0]
+    cas_rows = cas_table(points)
+    scaled_rows = cas_rows / points
+    pw_rank = lax.axis_index("pw")
+    kx_val = frequency(gsphere // (slab_rows * points), points)
+    ky_val = frequency(pw_rank * slab_rows + gsphere // points % slab_rows, points)
+    kz_val = frequency(gsphere % points, points)
+    kinetic = 8.0 * (kx_val * kx_val + ky_val * ky_val + kz_val * kz_val) / (points * points)
+
+    def gather_pw(value, axis=0):
+        return lax.all_gather(value, "pw", axis=axis, tiled=True)
+
+    slab_cells = points * slab_rows * points
+    owner = jnp.arange(ranks, dtype=jnp.int32)[:, None]
+    entry_count = ranks * sphere_dev
+    slab_pairs = slab_rows * points // LANES
+    all_pairs = ranks * slab_pairs
+    rows = perts * points
+
+    def by_x(value):
+        value = value.reshape(ranks, points, slab_pairs, -1)
+        return value.transpose(1, 0, 2, 3).reshape(points, all_pairs, -1)
+
+    slab_count = slab_cells // LANES
+    first_cells = jnp.arange(slab_count, dtype=jnp.int32) * LANES
+    starts = jnp.sum((gsphere[None, :] < first_cells[:, None]).astype(jnp.int32), axis=1)
+    bases = starts // LANES * LANES
+    placed = (
+        jnp.full((slab_cells,), -1, jnp.int32)
+        .at[gsphere]
+        .set(
+            jnp.arange(sphere_dev, dtype=jnp.int32),
+            unique_indices=True,
+            indices_are_sorted=True,
+        )
+    ).reshape(slab_count, LANES)
+    placed = jnp.where(placed < 0, -1, placed - bases[:, None])
+    place = by_x(gather_pw(placed))
+    base = by_x(gather_pw(bases).reshape(ranks, -1) + owner * sphere_dev)[:, :, 0]
+    block = by_x(jnp.arange(ranks * slab_count, dtype=jnp.int32))[:, :, 0]
+    entries = (gather_pw(gsphere).reshape(ranks, sphere_dev) + owner * slab_cells).reshape(1, -1)
+    entries = jnp.pad(entries, ((0, 0), (0, 2 * LANES)), constant_values=-1)
+    entries = jnp.broadcast_to(entries, (8, entry_count + 2 * LANES))
+    all_pot = gather_pw(local_pot).reshape(points, points, 1, points)
+    all_pot = jnp.tile(all_pot, (1, 1, perts, NB)).reshape(points, rows, lanes)
+    all_beta = gather_pw(beta_proj)
+    all_coef = gather_pw(proj_coef)
+    lines = beta_proj.shape[1] // points
+    slab_blocks = slab_rows * points // lines
+    pick = gather_pw(pblock)
+    proj_dev = pblock.shape[0]
+    proj_block = (pick.reshape(ranks, proj_dev) + owner * slab_blocks).reshape(-1)
+    beta_lines = jnp.tile(all_beta.reshape(-1, lines, 1, points), (1, 1, perts, NB))
+    beta_lines = beta_lines.reshape(-1, lines * perts, lanes)
+    one_hot = (
+        pick.reshape(ranks, 1, proj_dev)
+        == jnp.arange(slab_blocks, dtype=jnp.int32)[None, :, None]
+    ).astype(jnp.bfloat16)
+
+    def pair(matrix):
+        return jnp.kron(jnp.eye(NB, dtype=jnp.float32), matrix)
+
+    def each_pert(matrix, count):
+        return jnp.kron(matrix, jnp.eye(count, dtype=jnp.float32))
+
+    def box_of(coeffs):
+        coeffs = jnp.pad(coeffs.astype(jnp.float32), ((0, 0), (0, 2 * LANES)))
+        return expand(base, place, coeffs).reshape(points, rows, lanes)
+
+    def to_real(box):
+        count = box.shape[1] // points
+        box = jnp.einsum("xsm,mn->xsn", box, pair(cas_rows), precision=MID)
+        box = jnp.einsum("xsm,sg->xgm", box, each_pert(cas_rows, count), precision=MID)
+        return jnp.einsum("xsm,xg->gsm", box, cas_rows, precision=MID)
+
+    def to_sphere(field):
+        box = jnp.einsum("xsm,xg->gsm", field, scaled_rows, precision=MID)
+        box = jnp.einsum("xsm,sg->xgm", box, each_pert(scaled_rows, perts), precision=MID)
+        box = jnp.einsum("xsm,mn->xsn", box, pair(scaled_rows), precision=MID)
+        box = box.reshape(points, all_pairs, 8, LANES)
+        return compress(base, block, entries, box)[:, :entry_count]
+
+    def spread(coeffs):
+        return lax.all_to_all(coeffs.astype(SENT), "pw", split_axis=0, concat_axis=1, tiled=True)
+
+    def collect(coeffs):
+        return lax.all_to_all(
+            coeffs.astype(SENT), "pw", split_axis=1, concat_axis=0, tiled=True
+        )
+
+    def correlations(coeffs):
+        part = lax.dot_general(
+            coeffs.astype(jnp.bfloat16),
+            band_panel,
+            (((1,), (1,)), ((), ())),
+            preferred_element_type=jnp.float32,
+        )
+        return lax.psum(part, "pw")
+
+    def occupied(over_b):
+        return jnp.dot(over_b, band_panel, preferred_element_type=jnp.float32)
+
+    def residual_norm(residual):
+        return lax.psum(jnp.sum(residual * residual, axis=1), "pw")
+
+    same_band = pair(jnp.ones((points, points), jnp.float32))
+
+    def nonlocal_term(field):
+        picked = field.reshape(-1, lines * perts, lanes)[proj_block]
+        amp = jnp.sum((picked * beta_lines).reshape(-1, lines, perts, lanes), axis=1)
+        amp = jnp.einsum("qpm,mn->qpn", amp, same_band, precision=MID)
+        amp = jnp.tile(amp * all_coef[:, None, None], (1, lines, 1))
+        addition = (amp * beta_lines).reshape(ranks, proj_dev, lines * perts, lanes)
+        high = addition.astype(jnp.bfloat16)
+        low = (addition - high.astype(jnp.float32)).astype(jnp.bfloat16)
+        added = sum(
+            jnp.einsum("dbq,dqsm->dbsm", one_hot, part, preferred_element_type=jnp.float32)
+            for part in (high, low)
+        )
+        return added.reshape(field.shape)
+
+    first_bands = gather_pw(band_panel[:NB], axis=1)
+    band_box = box_of(jnp.repeat(first_bands, perts, axis=0))
+    band_box = band_box.reshape(points, points, perts, lanes)[:, :, 0]
+    bands_real = to_real(band_box)
+    every_band = jnp.repeat(bands_real, perts, axis=1)
+    pert_whole = lax.all_to_all(dvpert, "pw", split_axis=0, concat_axis=1, tiled=True)
+    pert_cells = pert_whole.reshape(perts, points, points, points).transpose(1, 2, 0, 3)
+    pert_cells = jnp.tile(pert_cells.astype(jnp.float32), (1, 1, 1, NB))
+    products = pert_cells.reshape(points, rows, lanes) * every_band
+    sent_source = collect(to_sphere(products))
+    source = sent_source.astype(jnp.float32)
+    every_source = lax.all_gather(
+        sent_source.astype(jnp.bfloat16), "img", axis=0, tiled=True
+    )
+    source_over = correlations(source).astype(jnp.bfloat16)
+    right_side = occupied(source_over) - source
+    eps_rows = jnp.tile(jnp.repeat(eps_band, perts), ranks)
+    change = jnp.zeros_like(right_side)
+    residual = right_side
+    direction = right_side
+    norm_now = residual_norm(residual)
+    for iteration in range(ITERS):
+        correlation = correlations(direction)
+        field_real = to_real(box_of(spread(direction)))
+        potential = all_pot * field_real + nonlocal_term(field_real)
+        applied = collect(to_sphere(potential)).astype(jnp.float32)
+        shifted = applied + (kinetic[None] - eps_rows[:, None]) * direction
+        curvature = lax.psum(jnp.sum(direction * shifted, axis=1), "pw")
+        over_b = correlation.astype(jnp.bfloat16)
+        curvature = curvature + ALPHA_PV * jnp.sum(correlation * over_b.astype(jnp.float32), axis=1)
+        product_vec = shifted + ALPHA_PV * occupied(over_b)
+        step_len = norm_now / curvature
+        change = change + step_len[:, None] * direction
+        if iteration + 1 < ITERS:
+            residual = residual - step_len[:, None] * product_vec
+            norm_next = residual_norm(residual)
+            direction = residual + (norm_next / (norm_now + SHIFT_EPS))[:, None] * direction
+            norm_now = norm_next
+    response = to_real(box_of(spread(change))) * every_band
+    density = 4.0 * jnp.sum(response.reshape(points, points, perts, NB, points), axis=3)
+    density = density.astype(SENT).transpose(2, 0, 1, 3)
+    density = density.reshape(perts, points, points * points)
+    density_resp = lax.all_to_all(density, "pw", split_axis=1, concat_axis=0, tiled=True)
+    every_source = every_source.reshape(-1, NB, perts, sphere_dev)
+    change_high = change.astype(jnp.bfloat16)
+    change_low = (change - change_high.astype(jnp.float32)).astype(jnp.bfloat16)
+    chi_part = sum(
+        lax.dot_general(
+            every_source[:, band].reshape(-1, sphere_dev),
+            part.reshape(ranks, NB, perts, sphere_dev)[:, band].reshape(pert_dev, sphere_dev),
+            (((1,), (1,)), ((), ())),
+            preferred_element_type=jnp.float32,
+        )
+        for band in range(NB)
+        for part in (change_high, change_low)
+    )
+    chi_matrix = 4.0 * lax.psum(chi_part, "pw")
+    return (density_resp.astype(jnp.float32), chi_matrix)
+
+
 def solution(mesh):
     return jax.shard_map(
         local,

time: 3320 us -> 1750 us (0.53)
  local copies, waits for them, and re-layouts: 1120 us -> 443 us
  Pallas kernels: 0 us -> 492 us
  blocking collectives: 622 us -> 190 us
  other arithmetic: 508 us -> 134 us
  waiting for transfers between devices: 514 us -> 144 us
  matrix products: 498 us -> 286 us
    all_to_all x3 -> x0, blocking collectives: 564 us -> none  [the longest x2 374 us: to_real(): lax.all_to_all(along_x, 'pw', split_axis=1, concat_axis=2, tiled=True)]
    pallas_call x0 -> x7, Pallas kernels: none -> 492 us  [the longest x3 267 us: compress(): pl.pallas_call(compress_kernel, grid=(points // STEP_X,), in_specs=[pl.Bl...]
    all_to_all x4 -> x8, waiting for transfers between devices: 407 us -> 73.7 us  [the longest x1 40.1 us: local(): lax.all_to_all(density, 'pw', split_axis=1, concat_axis=0, tiled=True)]
    scatter-add x2 -> x0, other arithmetic: 269 us -> none  [local(): jnp.zeros_like(blocks).at[:, pblock, :].add(addition)]
    dot_general x27 -> x36, matrix products: 498 us -> 286 us  [the longest x3 45 us: correlations(): lax.dot_general(coeffs.astype(jnp.bfloat16), band_panel, (((1,), (1,)), (...]
    unnamed x85 -> x90, local copies, waits for them, and re-layouts: 193 us -> 2.6 us
    all_to_all x7 -> x2, other arithmetic: 171 us -> 4.38 us  [spread(): lax.all_to_all(coeffs.astype(SENT), 'pw', split_axis=0, concat_axis=1, ti...]
    gather x8 -> x2, local copies, waits for them, and re-layouts: 224 us -> 68.7 us  [nonlocal_term(): picked = field.reshape(-1, lines * perts, lanes)[proj_block]]
  transfers between devices with their start and end apart: 7 -> 14, of which waited for: 6 -> 6; matrix products, arithmetic and copies ran while one was open for 14% -> 22% of each run, Pallas kernels for 0% -> 12%
where the time goes in v1:
time: 1750 us; the launch traced here: 1740 us
  Pallas kernels  492 us (28%)
  local copies, waits for them, and re-layouts  443 us (25%)
  matrix products  286 us (16%)
  blocking collectives  190 us (11%)
  waiting for transfers between devices  144 us (8%)
  other arithmetic  134 us (8%)
  starting transfers between devices  34.9 us (2%)
    pallas_call x3, Pallas kernels, compress(): pl.pallas_call(compress_kernel, grid=(points // STEP_X,), in_specs=[pl.Bl...  267 us
    pallas_call x4, Pallas kernels, expand(): pl.pallas_call(expand_kernel, grid=(points // STEP_X,), in_specs=[pl.Bloc...  225 us
    all_gather x5, blocking collectives, gather_pw(): return lax.all_gather(value, 'pw', axis=axis, tiled=True)  126 us
    another operation x6, local copies, waits for them, and re-layouts, local(): jnp.tile(all_beta.reshape(-1, lines, 1, points), (1, 1, perts, NB))  74.8 us
    psum x2, waiting for transfers between devices, correlations(): return lax.psum(part, 'pw')  69.4 us
    gather x2, local copies, waits for them, and re-layouts, nonlocal_term(): picked = field.reshape(-1, lines * perts, lanes)[proj_block]  68.7 us
    scatter x1, local copies, waits for them, and re-layouts, local(): placed = jnp.full((slab_cells,), -1, jnp.int32).at[gsphere].set(jnp.arang...  52.9 us
    dot_general x3, matrix products, correlations(): lax.dot_general(coeffs.astype(jnp.bfloat16), band_panel, (((1,), (1,)), (...  45 us
  transfers between devices with their start and end apart: 14, of which 6 were waited for; matrix products, arithmetic and copies ran while one was open for 22% of the time, Pallas kernels for 12%

profile of v1, /device:TPU:0, one launch (start us, length us, event | category | flops | bytes accessed | tf_op | source)
XLA Modules:
  0.0 1740.3 jit_solution(394608804209932561)
XLA Ops:
  12.0 52.9 %scatter_custom_fusion = s32[65536]{0:T(1024)S(1)} fusion(s32[14336]{0:T(1024)S(1)} %add_select_fusion.4, s32[14336]{0:T(1024)S(1)} %iota.215, s32[]{:T(128)} %constant.111.clone.1), kind=kCustom, calls=%fused_computation.126 | custom fusion | bytes 262148 | tf_op jit(solution)/shard_map/scatter | solution.py:271
  72.9 69.6 %all-gather = s32[4,1,512]{2,1,0:T(1,128)S(1)} all-gather(s32[1,1,512]{2,1,0:T(1,128)S(1)} %bitcast.258), channel_id=1, replica_groups=mesh['img'=8,'pw'=4] {'pw'}, dimensions={0}, use_global_device_ids=true | all-gather | bytes 10240 | tf_op jit(solution)/shard_map/all_gather | solution.py:251
  143.9 15.2 all_gather.30
  179.9 14.3 all_gather.29
  196.9 56.2 %shard_map.95 = f32[64,32,8,128]{3,2,1,0:T(8,128)S(1)} custom-call(s32[64,32]{1,0:T(8,128)S(1)} %copy.252.base_ref, s32[64,32,128]{2,1,0:T(8,128)S(1)} %bitcast.225, f32[8,57600]{1,0:T(8,128)S(1)} %pad.24.coeffs_ref), custom_call_target="tpu_custom_call" | custom-call | tf_op jit(solution)/shard_map/pallas_call | solution.py:199
  272.5 11.5 copy.210
  293.0 16.5 tile.58
  330.8 89.2 %shard_map.96 = f32[8,57600]{1,0:T(8,128)S(1)} custom-call(s32[64,32]{1,0:T(8,128)S(1)} %copy.252.base_ref, s32[64,32]{1,0:T(8,128)S(1)} %copy.219.block_ref, s32[8,57600]{1,0:T(8,128)S(1)} %broadcast_in_dim.86.entry_ref, f32[64,32,8,128]{3,2,1,0:T(8,128)S(1)} %fusion.7.box_ref), custom_call_target="tpu_custom_call" | custom-call | tf_op jit(solution)/shard_map/pallas_call | solution.py:215
  425.6 17.5 %all-to-all-done.1 = bf16[8,4,14336]{2,0,1:T(8,128)(2,1)S(1)} async-done(((bf16[8,4,14336]{2,0,1:T(8,128)(2,1)}), bf16[8,4,14336]{2,0,1:T(8,128)(2,1)S(1)}, u32[]{:S(2)}, u32[]{:S(2)}) %all-to-all-start.1) | async-done | bytes 917536 | tf_op jit(solution)/shard_map/all_to_all | solution.py:327
  443.0 14.5 fusion.132
  457.6 25.2 %all-reduce.13 = bf16[32,1024]{1,0:T(8,128)(2,1)S(1)} all-reduce(f32[32,1024]{1,0:T(8,128)S(1)} %fusion.132), channel_id=1, replica_groups=mesh['img'=8,'pw'=4] {'pw'}, use_global_device_ids=true, to_apply=%region_2.3 | all-reduce | flops 32768 | bytes 196608 | tf_op jit(solution)/shard_map/psum | solution.py:338
  482.8 12.0 convolution_subtract_fusion
  510.6 13.6 all_gather.32
  524.8 13.1 all_gather.34
  550.2 16.4 tile.61
  586.1 20.4 %tile.69 = f32[4,1024,8,128]{1,0,3,2:T(4,128)} reshape(f32[4096,2,4,2,64]{0,4,3,2,1:T(8,128)} %tile.68) | data formatting | bytes 33554432 | tf_op jit(solution)/shard_map/tile | solution.py:293
  606.5 19.5 %copy.228 = f32[4,1024,8,128]{3,1,0,2:T(8,128)} copy(f32[4,1024,8,128]{1,0,3,2:T(4,128)} %tile.69) | data formatting | bytes 33554432 | tf_op jit(solution)/shard_map/tile | solution.py:293
  627.3 56.2 %shard_map.97 = f32[64,32,8,128]{3,2,1,0:T(8,128)S(1)} custom-call(s32[64,32]{1,0:T(8,128)S(1)} %copy.252.base_ref, s32[64,32,128]{2,1,0:T(8,128)S(1)} %bitcast.226, f32[8,57600]{1,0:T(8,128)S(1)} %pad_convert_fusion.2.coeffs_ref), custom_call_target="tpu_custom_call" | custom-call | tf_op jit(solution)/shard_map/pallas_call | solution.py:199
  693.4 12.6 fusion.37
  714.1 34.3 %gather_fusion = f32[4096,8,128]{2,1,0:T(8,128)} fusion(f32[2048,8,128]{2,1,0:T(8,128)} %bitcast.235, s32[4096]{0:T(1024)S(1)} %copy-done.34), kind=kCustom, calls=%fused_computation | custom fusion | bytes 33570816 | tf_op jit(solution)/shard_map/gather | solution.py:349
  748.5 14.1 multiply_reduce_fusion.1
  779.3 15.4 multiply_convert_fusion.1
  812.8 11.5 copy.231
  824.3 17.9 %fusion.30 = f32[64,256,128]{2,0,1:T(8,128)} fusion(f32[64,256,128]{2,1,0:T(8,128)} %bitcast.242, f32[64,256,128]{2,0,1:T(8,128)S(1)} %bitcast.231, f32[64,256,128]{2,0,1:T(8,128)} %copy-done.6), kind=kOutput, calls=%fused_computation.45 | convolution fusion | flops 809566208 | bytes 33554432 | tf_op jit(solution)/shard_map/xsm,xg->gsm/dot_general | solution.py:317
  842.2 12.2 fusion.28
  857.9 89.2 %shard_map.98 = f32[8,57600]{1,0:T(8,128)S(1)} custom-call(s32[64,32]{1,0:T(8,128)S(1)} %copy.252.base_ref, s32[64,32]{1,0:T(8,128)S(1)} %copy.219.block_ref, s32[8,57600]{1,0:T(8,128)S(1)} %copy-done.1, f32[64,32,8,128]{3,2,1,0:T(8,128)S(1)} %fusion.5.box_ref), custom_call_target="tpu_custom_call" | custom-call | tf_op jit(solution)/shard_map/pallas_call | solution.py:215
  952.7 15.0 fusion.82
  968.1 34.1 %all-reduce.10.cloned.1.call-done = f32[32,1024]{1,0:T(8,128)} async-done(((f32[32,1024]{1,0:T(8,128)}), f32[32,1024]{1,0:T(8,128)}) %all-reduce.10.cloned.1.call-update) | async-done | bytes 131088 | tf_op jit(solution)/shard_map/psum | solution.py:338
  1015.6 16.2 multiply_reduce_fusion.2
  1048.0 15.4 copy.243
  1067.0 56.2 %shard_map.99 = f32[64,32,8,128]{3,2,1,0:T(8,128)S(1)} custom-call(s32[64,32]{1,0:T(8,128)S(1)} %copy.252.base_ref, s32[64,32,128]{2,1,0:T(8,128)S(1)} %bitcast.227, f32[8,57600]{1,0:T(8,128)S(1)} %pad_convert_fusion.1.coeffs_ref), custom_call_target="tpu_custom_call" | custom-call | tf_op jit(solution)/shard_map/pallas_call | solution.py:199
  1132.8 12.5 fusion.26
  1153.5 34.4 %gather_fusion.1 = f32[4096,8,128]{2,1,0:T(8,128)} fusion(f32[2048,8,128]{2,1,0:T(8,128)} %bitcast.234, s32[4096]{0:T(1024)S(1)} %copy-done.34), kind=kCustom, calls=%fused_computation.1 | custom fusion | bytes 33570816 | tf_op jit(solution)/shard_map/gather | solution.py:349
  1187.9 14.1 multiply_reduce_fusion
  1218.8 18.9 %fusion.54 = (bf16[4,1024,8,128]{3,2,1,0:T(8,128)(2,1)}, bf16[4,1024,8,128]{3,2,1,0:T(8,128)(2,1)S(1)}) fusion(f32[4,1024,8,128]{3,2,1,0:T(8,128)} %copy.243, f32[4,1024,8,128]{3,1,0,2:T(8,128)} %bitcast.237), kind=kLoop, calls=%fused_computation.64 | loop fusion | flops 20971520 | bytes 50331648 | tf_op jit(solution)/shard_map/convert_element_type | solution.py:354
  1244.5 11.8 fusion.67
  1267.8 18.0 %fusion.19 = f32[64,256,128]{2,0,1:T(8,128)} fusion(f32[64,256,128]{2,1,0:T(8,128)} %bitcast.241, f32[64,256,128]{2,0,1:T(8,128)S(1)} %bitcast.233, f32[64,256,128]{2,0,1:T(8,128)} %copy-done.5), kind=kOutput, calls=%fused_computation.33 | convolution fusion | flops 809566208 | bytes 33554432 | tf_op jit(solution)/shard_map/xsm,xg->gsm/dot_general | solution.py:317
  1285.8 12.2 fusion.17
  1301.5 89.2 %shard_map.100 = f32[8,57600]{1,0:T(8,128)S(1)} custom-call(s32[64,32]{1,0:T(8,128)S(1)} %copy.252.base_ref, s32[64,32]{1,0:T(8,128)S(1)} %copy.219.block_ref, s32[8,57600]{1,0:T(8,128)S(1)} %copy-done.2, f32[64,32,8,128]{3,2,1,0:T(8,128)S(1)} %fusion.3.box_ref), custom_call_target="tpu_custom_call" | custom-call | tf_op jit(solution)/shard_map/pallas_call | solution.py:215
  1396.0 15.5 fusion.80
  1412.1 35.3 %all-reduce.12.cloned.1.call-done = f32[32,1024]{1,0:T(8,128)} async-done(((f32[32,1024]{1,0:T(8,128)}), f32[32,1024]{1,0:T(8,128)}) %all-reduce.12.cloned.1.call-update) | async-done | bytes 131088 | tf_op jit(solution)/shard_map/psum | solution.py:338
  1475.5 13.8 all-to-all-done.6
  1489.4 56.2 %shard_map.101 = f32[64,32,8,128]{3,2,1,0:T(8,128)S(1)} custom-call(s32[64,32]{1,0:T(8,128)S(1)} %copy.252.base_ref, s32[64,32,128]{2,1,0:T(8,128)S(1)} %bitcast.228, f32[8,57600]{1,0:T(8,128)S(1)} %pad_convert_fusion.coeffs_ref), custom_call_target="tpu_custom_call" | custom-call | tf_op jit(solution)/shard_map/pallas_call | solution.py:199
  1553.3 14.3 bitcast_multiply_fusion
  1567.6 16.9 reshape.446
  1584.4 25.8 %reduce_sum.99 = f32[64,64,4,64]{3,0,2,1:T(8,128)} reduce(f32[64,64,4,2,64]{4,3,0,2,1:T(2,128)} %reshape.446, f32[]{:T(128)} %constant.117.clone.1), dimensions={3}, to_apply=%region_17.18 | reduce | flops 1048576 | bytes 12582916 | tf_op jit(solution)/shard_map/reduce_sum | solution.py:401
  1636.6 40.1 %all-to-all-done.7 = bf16[4,64,4096]{2,0,1:T(4,128)(2,1)S(1)} async-done(((bf16[4,64,4096]{2,0,1:T(4,128)(2,1)}), bf16[4,64,4096]{2,0,1:T(4,128)(2,1)S(1)}, u32[]{:S(2)}, u32[]{:S(2)}) %all-to-all-start.7) | async-done | bytes 2097184 | tf_op jit(solution)/shard_map/all_to_all | solution.py:404
  1680.7 11.7 reshape.448
  (243 shorter events, 406.3 us)
Async XLA Ops:
  7.2 188.4 %all-gather.6.cloned.1.call-start = ((), (), s32[]{:S(2)}) async-start(), calls=%async_computation.8 | async-start | bytes 1310720 | tf_op jit(solution)/shard_map/all_gather | solution.py:251
  65.8 193.4 %all-to-all-start = ((bf16[16,16,4096]{2,1,0:T(8,128)(2,1)}), bf16[16,16,4096]{2,1,0:T(8,128)(2,1)}, u32[]{:S(2)}, u32[]{:S(2)}) async-start(bf16[16,16,4096]{2,1,0:T(8,128)(2,1)} %param.12), calls=%async_computation | async-start | bytes 4194304 | tf_op jit(solution)/shard_map/all_to_all | solution.py:367
  72.1 466.5 %all-gather.8.cloned.1.call-start = ((), (), s32[]{:S(2)}) async-start(), calls=%async_computation.9 | async-start | bytes 1310720 | tf_op jit(solution)/shard_map/all_gather | solution.py:251
  161.9 521.6 %copy-start.21 = (f32[128,128,1]{1,0,2:T(8,128)}, f32[128,128,1]{1,0,2:T(8,128)S(1)}, u32[]{:S(2)}) copy-start(f32[128,128,1]{1,0,2:T(8,128)S(1)} %reshape.487) | copy-start | bytes 196612
  169.0 10.9 copy-start.32
  177.3 141.2 %copy-start.12 = (f32[256,256]{1,0:T(8,128)}, f32[256,256]{1,0:T(8,128)S(1)}, u32[]{:S(2)}) copy-start(f32[256,256]{1,0:T(8,128)S(1)} %mul.676) | copy-start | bytes 786436
  259.2 50.4 %copy-start.9 = (f32[64,64,128]{2,0,1:T(8,128)}, f32[64,64,128]{2,0,1:T(8,128)S(1)}, u32[]{:S(2)}) copy-start(f32[64,64,128]{2,0,1:T(8,128)S(1)} %fusion.72) | copy-start | bytes 6291460
  318.5 8.7 copy-start.25
  330.7 89.2 %copy-start = (s32[8,57600]{1,0:T(8,128)}, s32[8,57600]{1,0:T(8,128)S(1)}, u32[]{:S(2)}) copy-start(s32[8,57600]{1,0:T(8,128)S(1)} %broadcast_in_dim.86.entry_ref) | copy-start | bytes 5529604
  330.7 93.8 %copy-start.31 = (f32[1024,128]{1,0:T(8,128)S(1)}, f32[1024,128]{1,0:T(8,128)}, u32[]{:S(2)}) copy-start(f32[1024,128]{1,0:T(8,128)} %param.13) | copy-start | bytes 1572868
  420.9 22.1 %all-to-all-start.1 = ((bf16[8,4,14336]{2,0,1:T(8,128)(2,1)}), bf16[8,4,14336]{2,0,1:T(8,128)(2,1)S(1)}, u32[]{:S(2)}, u32[]{:S(2)}) async-start(bf16[8,4,14336]{2,0,1:T(8,128)(2,1)} %bitcast.24), calls=%async_computation.1 | async-start | bytes 1835008 | tf_op jit(solution)/shard_map/all_to_all | solution.py:327
  424.5 142.1 %all-gather.10.cloned.1.call-start = ((), (), s32[]{:S(2)}) async-start(), calls=%async_computation.10 | async-start | bytes 2621440 | tf_op jit(solution)/shard_map/all_gather | solution.py:251
  443.0 39.7 %copy-start.8 = (bf16[8,4,14336]{2,0,1:T(8,128)(2,1)}, bf16[8,4,14336]{2,0,1:T(8,128)(2,1)S(1)}, u32[]{:S(2)}) copy-start(bf16[8,4,14336]{2,0,1:T(8,128)(2,1)S(1)} %all-to-all-done.1) | copy-start | bytes 2752516
  496.0 14.6 copy-start.36
  496.0 28.8 %copy-start.37 = (f32[1024]{0:T(1024)S(1)}, f32[1024]{0:T(1024)}, u32[]{:S(2)}) copy-start(f32[1024]{0:T(1024)} %param.14) | copy-start | bytes 12292
  497.0 129.0 %all-to-all-start.2 = ((bf16[4,8,14336]{2,1,0:T(8,128)(2,1)}), bf16[4,8,14336]{2,1,0:T(8,128)(2,1)}, u32[]{:S(2)}, u32[]{:S(2)}) async-start(bf16[4,8,14336]{2,1,0:T(8,128)(2,1)} %convert_bitcast_fusion.2), calls=%async_computation.2 | async-start | bytes 1835008 | tf_op jit(solution)/shard_map/all_to_all | solution.py:324
  509.7 177.2 %copy-start.15 = (f32[256,256]{1,0:T(8,128)}, f32[256,256]{1,0:T(8,128)S(1)}, u32[]{:S(2)}) copy-start(f32[256,256]{1,0:T(8,128)S(1)} %mul.669) | copy-start | bytes 786436
  538.0 224.6 %copy-start.23 = (f32[4096]{0:T(1024)}, f32[4096]{0:T(1024)S(1)}, u32[]{:S(2)}) copy-start(f32[4096]{0:T(1024)S(1)} %all_gather.34) | copy-start | bytes 49156
  566.6 11.5 copy-start.11
  706.0 8.1 copy-start.6
  748.5 14.1 copy-start.29
  779.3 15.4 copy-start.35
  779.3 45.0 %slice-start = ((s8[8388608]{0:T(1024)(128)(4,1)}), s8[4194304]{0:T(1024)(128)(4,1)S(1)}, s32[]{:S(2)}) async-start(s8[8388608]{0:T(1024)(128)(4,1)} %bitcast.230), calls=%async_computation.14 | async-start | bytes 8388608
  794.8 29.6 %slice-start.1 = ((s8[8388608]{0:T(1024)(128)(4,1)}), s8[4194304]{0:T(1024)(128)(4,1)S(1)}, s32[]{:S(2)}) async-start(s8[8388608]{0:T(1024)(128)(4,1)} %bitcast.230), calls=%async_computation.15 | async-start | bytes 8388608
  824.3 17.9 %copy-start.13 = (f32[256,256]{1,0:T(8,128)S(1)}, f32[256,256]{1,0:T(8,128)}, u32[]{:S(2)}) copy-start(f32[256,256]{1,0:T(8,128)} %copy-done.12) | copy-start | bytes 786436
  842.2 12.3 copy-start.26
  857.9 94.8 %copy-start.4 = (f32[32,14336]{1,0:T(8,128)S(1)}, f32[32,14336]{1,0:T(8,128)}, u32[]{:S(2)}) copy-start(f32[32,14336]{1,0:T(8,128)} %copy-done.3) | copy-start | bytes 5505028
  948.1 55.2 %all-to-all-start.3 = ((bf16[8,4,14336]{2,0,1:T(8,128)(2,1)}), bf16[8,4,14336]{2,0,1:T(8,128)(2,1)}, u32[]{:S(2)}, u32[]{:S(2)}) async-start(bf16[8,4,14336]{2,0,1:T(8,128)(2,1)} %bitcast.252), calls=%async_computation.3 | async-start | bytes 1835008 | tf_op jit(solution)/shard_map/all_to_all | solution.py:327
  952.7 15.0 copy-start.33
  952.7 15.2 copy-start.38
  952.7 49.6 %all-reduce.10.cloned.1.call-start = ((), (), s32[]{:S(2)}) async-start(), calls=%async_computation.11 | async-start | bytes 262144 | tf_op jit(solution)/shard_map/psum | solution.py:338
  1043.6 22.1 %all-to-all-start.4 = ((bf16[4,8,14336]{2,1,0:T(8,128)(2,1)}), bf16[4,8,14336]{2,1,0:T(8,128)(2,1)}, u32[]{:S(2)}, u32[]{:S(2)}) async-start(bf16[4,8,14336]{2,1,0:T(8,128)(2,1)} %get-tuple-element.8), calls=%async_computation.4 | async-start | bytes 1835008 | tf_op jit(solution)/shard_map/all_to_all | solution.py:324
  1063.4 59.8 %copy-start.22 = (f32[128,128,1]{1,0,2:T(8,128)S(1)}, f32[128,128,1]{1,0,2:T(8,128)}, u32[]{:S(2)}) copy-start(f32[128,128,1]{1,0,2:T(8,128)} %copy-done.21) | copy-start | bytes 196612
  1187.9 14.1 copy-start.24
  1187.9 14.1 copy-start.30
  1237.7 30.0 %slice-start.2 = ((s8[8388608]{0:T(1024)(128)(4,1)}), s8[4194304]{0:T(1024)(128)(4,1)S(1)}, s32[]{:S(2)}) async-start(s8[8388608]{0:T(1024)(128)(4,1)} %bitcast.232), calls=%async_computation.16 | async-start | bytes 8388608
  1244.5 23.3 %slice-start.3 = ((s8[8388608]{0:T(1024)(128)(4,1)}), s8[4194304]{0:T(1024)(128)(4,1)S(1)}, s32[]{:S(2)}) async-start(s8[8388608]{0:T(1024)(128)(4,1)} %bitcast.232), calls=%async_computation.17 | async-start | bytes 8388608
  1267.8 18.0 %copy-start.14 = (f32[256,256]{1,0:T(8,128)S(1)}, f32[256,256]{1,0:T(8,128)}, u32[]{:S(2)}) copy-start(f32[256,256]{1,0:T(8,128)} %copy-done.12) | copy-start | bytes 786436
  1285.8 12.3 copy-start.27
  1391.7 56.8 %all-to-all-start.5 = ((bf16[8,4,14336]{2,0,1:T(8,128)(2,1)}), bf16[8,4,14336]{2,0,1:T(8,128)(2,1)}, u32[]{:S(2)}, u32[]{:S(2)}) async-start(bf16[8,4,14336]{2,0,1:T(8,128)(2,1)} %bitcast.251), calls=%async_computation.5 | async-start | bytes 1835008 | tf_op jit(solution)/shard_map/all_to_all | solution.py:327
  1395.9 51.5 %all-reduce.12.cloned.1.call-start = ((), (), s32[]{:S(2)}) async-start(), calls=%async_computation.12 | async-start | bytes 262144 | tf_op jit(solution)/shard_map/psum | solution.py:338
  1411.5 269.1 %all-gather.12.cloned.1.call-start = ((), (), s32[]{:S(2)}) async-start(), calls=%async_computation.13 | async-start | bytes 8257536 | tf_op jit(solution)/shard_map/all_gather | solution.py:373
  1466.2 23.0 %all-to-all-start.6 = ((bf16[4,8,14336]{2,1,0:T(8,128)(2,1)}), bf16[4,8,14336]{2,1,0:T(8,128)(2,1)S(1)}, u32[]{:S(2)}, u32[]{:S(2)}) async-start(bf16[4,8,14336]{2,1,0:T(8,128)(2,1)} %bitcast.249), calls=%async_computation.6 | async-start | bytes 1835008 | tf_op jit(solution)/shard_map/all_to_all | solution.py:324
  1614.8 15.6 copy-start.17
  1626.6 50.1 %all-to-all-start.7 = ((bf16[4,64,4096]{2,0,1:T(4,128)(2,1)}), bf16[4,64,4096]{2,0,1:T(4,128)(2,1)S(1)}, u32[]{:S(2)}, u32[]{:S(2)}) async-start(bf16[4,64,4096]{2,0,1:T(4,128)(2,1)} %reshape.502), calls=%async_computation.7 | async-start | bytes 4194304 | tf_op jit(solution)/shard_map/all_to_all | solution.py:404
  1701.8 12.3 copy-start.18
  1701.8 15.5 copy-start.20
  1708.0 13.6 copy-start.19
  (9 other events, 41.8 us)
Sparse Core Ops, SparseCore 0:
  65.9 47.1 all-gather.5
  114.7 45.6 all-gather.7
  426.9 51.7 all-gather.9
  967.8 34.3 all-reduce.9
  1411.6 35.7 all-reduce.11
  1449.2 49.6 all-gather.11
